TPU v7x, 512 devices: a whole 4x4x16 slice. The times are simulated.
512 devices in a mesh: agent: 16 (over x, y), dp: 32 (over z, core).
Axes of the slice: x: 4, y: 4, z: 16, core: 2. Of those that a mesh axis runs over, the one named last changes fastest.
Arguments:
- learn_obs: bfloat16 [16, 1024, 16, 3456], P('agent', 'dp'), may hold values from -6 to 6
- own_obs: bfloat16 [16, 1024, 3456], P('agent', 'dp'), may hold values from -6 to 6
- opp_obs: bfloat16 [16, 1024, 3456], P('agent', 'dp'), may hold values from -6 to 6
- opponent: int32 [16, 1024, 1], P('agent', 'dp'), may hold values from 0 to 15; in each aligned block of 32 rows (0 to 31, 32 to 63, ..., all dimensions but the last counted through in order) at most 8 rows name the same one
- actions: int32 [16, 1024, 16], P('agent', 'dp'), may hold values from 0 to 17
- done: int32 [16, 1024, 16], P('agent', 'dp'), may hold values 0 or 1
- rewards: float32 [16, 1024, 16], P('agent', 'dp'), may hold values from -6 to 6
- behaviour: float32 [16, 1024, 16], P('agent', 'dp'), may hold values from -4.5 to -1.5
- core_master: float32 [16, 256, 3712], P('agent', 'dp'), may hold values from -0.109375 to 0.109375
- core_mom: float32 [16, 256, 3712], P('agent', 'dp'), may hold values from -6 to 6
- core_vel: float32 [16, 256, 3712], P('agent', 'dp'), may hold values from 0.1 to 1
- head_master: float32 [16, 19, 256], P('agent'), may hold values from -0.375 to 0.375
- head_mom: float32 [16, 19, 256], P('agent'), may hold values from -6 to 6
- head_vel: float32 [16, 19, 256], P('agent'), may hold values from 0.1 to 1
- rates: float32 [16], P('agent'), may hold values from 0.01 to 0.1
Outputs:
- own_logits: float32 [16, 1024, 18], P('agent', 'dp')
- opp_logits: bfloat16 [16, 1024, 18], P('agent', 'dp')
- new_core: float32 [16, 256, 3712], P('agent', 'dp')
- new_core_mom: float32 [16, 256, 3712], P('agent', 'dp')
- new_core_vel: float32 [16, 256, 3712], P('agent', 'dp')
- new_head: float32 [16, 19, 256], P('agent')
- new_head_mom: float32 [16, 19, 256], P('agent')
- new_head_vel: float32 [16, 19, 256], P('agent')
Inputs may be any that keep to these rules, and one draw needn't show every extreme that they name: Among the 32 environments of one device (aligned blocks of the environment dimension), at most 8 face the same opponent agent, and some device reaches 8 in every draw.
All inputs are finite; a program needn't handle non-finite values. No bound on the sum of `done` on one device may be relied on, other than what follows from the above.
Results may differ from a plain program's by a relative error of at most 0.023.
Values may be sent and summed in bfloat16 or wider, within the bound.
A program may use at most 64 MiB of HBM per device.

v0:
```python
import jax
import jax.numpy as jnp
from jax import lax
from jax.sharding import Mesh
from jax.sharding import PartitionSpec as P

BLOCK = 128
DP = ("dp_0", "dp_1")
gamma_rate = 0.99
baseline_cost = 0.5
entropy_cost = 0.05
beta_first = 0.9
beta_second = 0.99
adam_eps = 1e-08


def joined_along(blocks, dim):
    shape = list(blocks.shape[1:])
    shape[dim] *= blocks.shape[0]
    return jnp.moveaxis(blocks, 0, dim).reshape(shape)


def stacked_from(x, axes, order):
    blocks = x[None]
    for k in order:
        blocks = lax.all_gather(blocks, axes[k], axis=0, tiled=True)
    current = [lax.axis_size(axes[k]) for k in reversed(order)]
    blocks = blocks.reshape(*current, *x.shape)
    turned = sorted(range(len(order)), key=lambda place: order[len(order) - 1 - place])
    return blocks.transpose(*turned, *range(len(order), blocks.ndim)).reshape(-1, *x.shape)


def gather_axes(x, axes, order, dim):
    return joined_along(stacked_from(x, axes, order), dim)


def reduced_to_own(blocks, axes, order):
    shape = [lax.axis_size(a) for a in axes]
    blocks = blocks.reshape(*shape, *blocks.shape[1:])
    blocks = blocks.transpose(*order, *range(len(axes), blocks.ndim))
    blocks = blocks.reshape(-1, *blocks.shape[len(axes) :])
    for k in order:
        blocks = lax.psum_scatter(blocks, axes[k], scatter_dimension=0, tiled=True)
    return blocks[0]


def in_blocks(x, dim, peers):
    before, after = (x.shape[:dim], x.shape[dim + 1 :])
    return jnp.moveaxis(x.reshape(*before, peers, -1, *after), dim, 0)


def sum_by_axis(x, axes, order, dim):
    peers = lax.axis_size(axes)
    return reduced_to_own(in_blocks(x, dim, peers), axes, order)


def by_axis(x, axes):
    for axis in axes:
        x = lax.psum(x, axis)
    return x


def contract(left, right):
    return lax.dot_general(
        left, right, (((1,), (1,)), ((), ())), preferred_element_type=jnp.float32
    )


def contract_rows(left, right):
    return lax.dot_general(
        left, right, (((0,), (0,)), ((), ())), preferred_element_type=jnp.float32
    )


def forward(inputs, core_bf, head_bf):
    width = inputs.shape[-1]
    pre_one = contract(inputs, core_bf[:, :width])
    first_act = jax.nn.relu(pre_one)
    first_bf = first_act.astype(jnp.bfloat16)
    pre_two = contract(first_bf, core_bf[:, width:])
    second_act = jax.nn.relu(pre_two) + first_act
    second_bf = second_act.astype(jnp.bfloat16)
    network_outputs = contract(second_bf, head_bf)
    return (network_outputs, pre_one, first_bf, pre_two, second_bf)


def importance_trace_gradients(
    network_outputs, bootstrap_value, actions, done, rewards, behaviour, scale_factor
):
    action_count = network_outputs.shape[-1] - 1
    logits = network_outputs[..., :action_count]
    values = network_outputs[..., action_count]
    totals = jnp.sum(jnp.exp(logits), -1)
    logp = logits - jnp.log(totals)[..., None]
    probs = jnp.exp(logp)
    chosen = (actions[..., None] == jnp.arange(action_count, dtype=jnp.int32)).astype(jnp.float32)
    logp_act = jnp.sum(logp * chosen, -1)
    ratio = jnp.minimum(1.0, jnp.exp(logp_act - behaviour))
    discount = gamma_rate * (1.0 - done.astype(jnp.float32))
    next_values = jnp.concatenate([values[:, 1:], bootstrap_value[:, None]], 1)
    deltas = ratio * (rewards + discount * next_values - values)

    def backstep(carry, item):
        delta, factor = item
        carry = delta + factor * carry
        return (carry, carry)

    start = jnp.zeros((values.shape[0],), jnp.float32)
    final_carry, corrections = lax.scan(
        backstep, start, (deltas.T, (discount * ratio).T), reverse=True
    )
    targets = values + corrections.T
    next_targets = jnp.concatenate([targets[:, 1:], bootstrap_value[:, None]], 1)
    advantage = ratio * (rewards + discount * next_targets - values)
    entropy = -jnp.sum(probs * logp, -1)
    grad_logits = scale_factor * (
        -advantage[..., None] * (chosen - probs)
        + entropy_cost * probs * (logp + entropy[..., None])
    )
    grad_value = scale_factor * (-baseline_cost * (targets - values))
    return jnp.concatenate([grad_logits, grad_value[..., None]], -1)


def adam_step(master, moment, second, grad, rate):
    moment = beta_first * moment + (1.0 - beta_first) * grad
    second = beta_second * second + (1.0 - beta_second) * grad * grad
    master = master - rate * moment / (jnp.sqrt(second) + adam_eps)
    return (master, moment, second)


def per_device(
    learn_obs,
    own_obs,
    opp_obs,
    opponent,
    actions,
    done,
    rewards,
    behaviour,
    core_master,
    core_mom,
    core_vel,
    head_master,
    head_mom,
    head_vel,
    rates,
):
    environment_total, rollout_length, width = (
        learn_obs.shape[1],
        learn_obs.shape[2],
        learn_obs.shape[3],
    )
    action_count = head_master.shape[1] - 1
    agent_count = lax.axis_size("agent")
    slots = min(environment_total, BLOCK // agent_count)
    scale_factor = 1.0 / rollout_length
    core_bf = gather_axes(core_master.astype(jnp.bfloat16), DP, (0, 1), 1)[0]
    head_bf = head_master[0].astype(jnp.bfloat16)
    own_out = forward(own_obs[0], core_bf, head_bf)[0]
    ids = opponent[0, :, 0]
    earlier = (ids[None, :] == ids[:, None]) & jnp.tril(jnp.ones((ids.shape[0],) * 2, bool), -1)
    ranks = jnp.sum(earlier.astype(jnp.int32), 1)
    position = ids * slots + ranks
    placing = (
        position[None, :] == jnp.arange(agent_count * slots, dtype=jnp.int32)[:, None]
    ).astype(jnp.bfloat16)
    outgoing = jnp.dot(placing, opp_obs[0], preferred_element_type=jnp.float32).astype(jnp.bfloat16)
    outgoing = outgoing.reshape(agent_count, slots, width)
    incoming = lax.all_to_all(outgoing, "agent", split_axis=0, concat_axis=0, tiled=True)
    count = incoming.shape[1]
    played = forward(incoming.reshape(agent_count * count, width), core_bf, head_bf)[0][
        :, :action_count
    ]
    played = played.astype(jnp.bfloat16).reshape(agent_count, count, action_count)
    returned = lax.all_to_all(played, "agent", split_axis=0, concat_axis=0, tiled=True)
    opp_logits = returned.reshape(agent_count * slots, action_count)[position]
    rows = learn_obs[0].reshape(environment_total * rollout_length, width)
    network_outputs, pre_one, first_bf, pre_two, second_bf = forward(rows, core_bf, head_bf)
    output_gradient = importance_trace_gradients(
        network_outputs.reshape(environment_total, rollout_length, action_count + 1),
        own_out[:, action_count],
        actions[0],
        done[0],
        rewards[0],
        behaviour[0],
        scale_factor,
    )
    grad_bf = output_gradient.reshape(environment_total * rollout_length, action_count + 1).astype(
        jnp.bfloat16
    )
    head_grad = contract_rows(grad_bf, second_bf)
    grad_second = jnp.dot(grad_bf, head_bf, preferred_element_type=jnp.float32)
    grad_pre_two = jnp.where(pre_two > 0, grad_second, 0.0).astype(jnp.bfloat16)
    grad_first = grad_second + jnp.dot(
        grad_pre_two, core_bf[:, width:], preferred_element_type=jnp.float32
    )
    grad_pre_one = jnp.where(pre_one > 0, grad_first, 0.0).astype(jnp.bfloat16)
    core_grad = sum_by_axis(
        jnp.concatenate(
            [contract_rows(grad_pre_one, rows), contract_rows(grad_pre_two, first_bf)], 1
        ).astype(jnp.bfloat16),
        DP,
        (1, 0),
        0,
    ).astype(jnp.float32)
    head_total = by_axis(head_grad, DP)
    rate = rates[0]
    new_core, new_core_mom, new_core_vel = adam_step(
        core_master[0], core_mom[0], core_vel[0], core_grad, rate
    )
    new_head, new_head_mom, new_head_vel = adam_step(
        head_master[0], head_mom[0], head_vel[0], head_total, rate
    )
    return (
        own_out[:, :action_count][None],
        opp_logits[None],
        new_core[None],
        new_core_mom[None],
        new_core_vel[None],
        new_head[None],
        new_head_mom[None],
        new_head_vel[None],
    )


def solution(mesh):
    torus = Mesh(mesh.devices.reshape(mesh.shape["agent"], 16, 2), ("agent", "dp_0", "dp_1"))
    return jax.shard_map(
        per_device,
        mesh=torus,
        in_specs=(
            P("agent", DP, None, None),
            P("agent", DP, None),
            P("agent", DP, None),
            P("agent", DP, None),
            P("agent", DP, None),
            P("agent", DP, None),
            P("agent", DP, None),
            P("agent", DP, None),
            P("agent", DP, None),
            P("agent", DP, None),
            P("agent", DP, None),
            P("agent", None, None),
            P("agent", None, None),
            P("agent", None, None),
            P("agent"),
        ),
        out_specs=(
            P("agent", DP, None),
            P("agent", DP, None),
            P("agent", DP, None),
            P("agent", DP, None),
            P("agent", DP, None),
            P("agent", None, None),
            P("agent", None, None),
            P("agent", None, None),
        ),
        check_vma=False,
    )
```

profile of v0, /device:TPU:1, one launch (start us, length us, event | category | flops | bytes accessed | tf_op | source)
XLA Modules:
  0.0 268.0 jit_solution(14837776084978435782)
XLA Ops:
  8.3 37.6 %all-gather = bf16[16,8,3712]{2,1,0:T(8,128)(2,1)} all-gather(bf16[1,8,3712]{2,1,0:T(8,128)(2,1)S(1)} %convert_element_type.71), channel_id=2, replica_groups=mesh['agent'=16,'dp_0'=16,'dp_1'=2] {'dp_0'}, dimensions={0}, use_global_device_ids=true | all-gather | bytes 1009664 | tf_op jit(solution)/shard_map/all_gather | solution.py:26
  46.8 1.4 convert_element_type.81
  48.1 22.9 %all-gather.4.cloned.1.call-done = bf16[32,8,3712]{2,1,0:T(8,128)(2,1)} async-done(((bf16[16,8,3712]{2,1,0:T(8,128)(2,1)}), bf16[32,8,3712]{2,1,0:T(8,128)(2,1)}) %all-gather.4.cloned.1.call-update) | async-done | bytes 1900560 | tf_op jit(solution)/shard_map/all_gather | solution.py:26
  71.0 1.7 copy.180
  75.3 1.8 fusion.26
  77.1 2.6 fusion.4
  80.5 2.0 add_convert_fusion
  84.2 2.3 fusion.33
  89.7 1.3 fusion.71
  91.6 40.4 %while.17 = (s32[]{:T(128)}, f32[32]{0:T(128)}, f32[16,32]{1,0:T(8,128)}, f32[16,32]{1,0:T(8,128)}, f32[16,32]{1,0:T(8,128)}, /*index=5*/s32[]{:T(128)}, s32[]{:T(128)}, s32[]{:T(128)}) while((s32[]{:T(128)}, f32[32]{0:T(128)}, f32[16,32]{1,0:T(8,128)}, f32[16,32]{1,0:T(8,128)}, f32[16,32]{1,0:T(8,128)}, /*index=5*/s32[]{:T(128)}, ...), condition=%wide.region_4.5_spmd.clone, body=%wide.region_3.4_spmd.clone.sunk | while | flops 100 | bytes 891 | solution.py:109
  92.8 1.3 dynamic_update_slice.12
  95.4 1.3 dynamic_update_slice.12
  97.9 1.3 dynamic_update_slice.12
  100.4 1.3 dynamic_update_slice.12
  103.0 1.3 dynamic_update_slice.12
  105.5 1.3 dynamic_update_slice.12
  108.0 1.3 dynamic_update_slice.12
  110.5 1.3 dynamic_update_slice.12
  113.1 1.3 dynamic_update_slice.12
  115.6 1.3 dynamic_update_slice.12
  118.1 1.3 dynamic_update_slice.12
  120.7 1.3 dynamic_update_slice.12
  123.2 1.3 dynamic_update_slice.12
  125.7 1.3 dynamic_update_slice.12
  132.1 1.3 bitcast_add_fusion.1
  133.4 1.4 copy.188
  134.7 1.4 concatenate.38
  136.1 1.3 neg.13
  138.1 1.3 fusion.70
  140.2 1.9 fusion.31
  142.1 1.6 copy.189
  144.8 2.1 convolution_convert_fusion.2
  147.0 1.9 fusion.14
  148.9 1.8 copy.193
  150.7 2.1 convolution_convert_fusion
  152.9 1.4 copy.194
  155.2 2.2 fusion.3
  157.4 5.6 %all-to-all-start = ((bf16[16,8,3456]{2,1,0:T(8,128)(2,1)}), bf16[16,8,3456]{2,1,0:T(8,128)(2,1)}, u32[]{:S(2)}, u32[]{:S(2)}) async-start(bf16[16,8,3456]{2,1,0:T(8,128)(2,1)} %fusion.3), calls=%async_computation | async-start | bytes 1769472 | tf_op jit(solution)/shard_map/all_to_all | solution.py:169
  163.0 12.6 %reduce-scatter.5.cloned.1.call-done = bf16[16,8,3712]{2,1,0:T(8,128)(2,1)} async-done(((bf16[32,8,3712]{2,1,0:T(8,128)(2,1)}), bf16[16,8,3712]{2,1,0:T(8,128)(2,1)}) %reduce-scatter.5.cloned.1.call-update) | async-done | bytes 950288 | tf_op jit(solution)/shard_map/reduce_scatter | solution.py:43
  176.9 3.1 %fusion.15 = f32[128,256]{1,0:T(8,128)} fusion(bf16[256,3712]{1,0:T(8,128)(2,1)} %bitcast.156, bf16[16,8,3456]{2,1,0:T(8,128)(2,1)} %all-to-all-done), kind=kOutput, calls=%fused_computation.22 | convolution fusion | flops 226525184 | bytes 2785280 | tf_op jit(solution)/shard_map/dot_general | solution.py:64
  180.0 2.0 fusion.20
  182.0 1.4 copy.181
  183.4 5.7 %all-to-all-start.1 = ((bf16[16,8,18]{2,1,0:T(8,128)(2,1)}), bf16[16,8,18]{2,1,0:T(8,128)(2,1)}, u32[]{:S(2)}, u32[]{:S(2)}) async-start(bf16[16,8,18]{2,1,0:T(8,128)(2,1)} %bitcast.164), calls=%async_computation.1 | async-start | bytes 65536 | tf_op jit(solution)/shard_map/all_to_all | solution.py:175
  189.2 1.7 fusion.56
  190.9 45.8 %psum.14 = f32[19,256]{1,0:T(8,128)} all-reduce(f32[19,256]{1,0:T(8,128)} %fusion.56), channel_id=1, replica_groups=mesh['agent'=16,'dp_0'=16,'dp_1'=2] {'dp_0'}, use_global_device_ids=true, to_apply=%region_8.9 | all-reduce | flops 4864 | bytes 38912 | tf_op jit(solution)/shard_map/psum | solution.py:59
  236.7 17.5 %psum.15 = f32[19,256]{1,0:T(8,128)} all-reduce(f32[19,256]{1,0:T(8,128)} %psum.14), channel_id=1, replica_groups=mesh['agent'=16,'dp_0'=16,'dp_1'=2] {'dp_1'}, use_global_device_ids=true, to_apply=%region_9.10 | all-reduce | flops 4864 | bytes 38912 | tf_op jit(solution)/shard_map/psum | solution.py:59
  257.5 1.5 gather_fusion
  259.7 1.8 divide_subtract_fusion
  (80 shorter events, 41.3 us)
Async XLA Ops:
  7.2 69.9 %copy-start = (bf16[1,32,16,3456]{3,2,1,0:T(8,128)(2,1)S(1)}, bf16[1,32,16,3456]{3,2,1,0:T(8,128)(2,1)}, u32[]{:S(2)}) copy-start(bf16[1,32,16,3456]{3,2,1,0:T(8,128)(2,1)} %param.17) | copy-start | bytes 10616836
  7.2 63.8 %all-gather.4.cloned.1.call-start = ((), (), s32[]{:S(2)}) async-start(), calls=%async_computation.5 | async-start | bytes 2850816 | tf_op jit(solution)/shard_map/all_gather | solution.py:26
  46.0 129.6 %reduce-scatter.5.cloned.1.call-start = ((), (), s32[]{:S(2)}) async-start(), calls=%async_computation.4 | async-start | bytes 2850816 | tf_op jit(solution)/shard_map/reduce_scatter | solution.py:43
  46.8 37.5 %copy-start.7 = (s32[32,16]{1,0:T(8,128)}, s32[32,16]{1,0:T(8,128)S(1)}, u32[]{:S(2)}) copy-start(s32[32,16]{1,0:T(8,128)S(1)} %copy.182) | copy-start | bytes 6148
  71.0 3.0 %copy-start.12 = (bf16[1,32,3456]{2,1,0:T(8,128)(2,1)S(1)}, bf16[1,32,3456]{2,1,0:T(8,128)(2,1)}, u32[]{:S(2)}) copy-start(bf16[1,32,3456]{2,1,0:T(8,128)(2,1)} %param.18) | copy-start | bytes 663556
  72.7 1.3 copy-start.4
  77.1 6.1 %copy-start.8 = (bf16[1,19,256]{2,0,1:T(2,128)(2,1)S(1)}, bf16[1,19,256]{2,0,1:T(2,128)(2,1)}, u32[]{:S(2)}) copy-start(bf16[1,19,256]{2,0,1:T(2,128)(2,1)} %convert_element_type.81) | copy-start | bytes 29188
  79.7 0.8 copy-start.1
  82.5 0.7 copy-start.5
  143.7 3.3 %copy-start.2 = (f32[512,256]{1,0:T(8,128)S(1)}, f32[512,256]{1,0:T(8,128)}, u32[]{:S(2)}) copy-start(f32[512,256]{1,0:T(8,128)} %copy-done.1) | copy-start | bytes 1572868
  143.7 3.3 %copy-start.3 = (f32[512,256]{1,0:T(8,128)S(1)}, f32[512,256]{1,0:T(8,128)}, u32[]{:S(2)}) copy-start(f32[512,256]{1,0:T(8,128)} %get-tuple-element.223) | copy-start | bytes 1572868
  150.7 2.1 copy-start.6
  154.3 0.7 copy-start.11
  157.4 19.5 %all-to-all-start = ((bf16[16,8,3456]{2,1,0:T(8,128)(2,1)}), bf16[16,8,3456]{2,1,0:T(8,128)(2,1)}, u32[]{:S(2)}, u32[]{:S(2)}) async-start(bf16[16,8,3456]{2,1,0:T(8,128)(2,1)} %fusion.3), calls=%async_computation | async-start | bytes 1769472 | tf_op jit(solution)/shard_map/all_to_all | solution.py:169
  163.0 96.7 %reduce-scatter.7.cloned.1.call-start = ((), (), s32[]{:S(2)}) async-start(), calls=%async_computation.6 | async-start | bytes 1009664
  175.6 13.5 %copy-start.10 = (bf16[512,1]{0,1:T(2,128)(2,1)S(1)}, bf16[512,1]{0,1:T(2,128)(2,1)}, u32[]{:S(2)}) copy-start(bf16[512,1]{0,1:T(2,128)(2,1)} %concatenate.38) | copy-start | bytes 3076
  176.9 78.1 %copy-start.9 = (f32[32,19]{0,1:T(8,128)S(1)}, f32[32,19]{0,1:T(8,128)}, u32[]{:S(2)}) copy-start(f32[32,19]{0,1:T(8,128)} %fusion.26) | copy-start | bytes 7300
  183.4 74.1 %all-to-all-start.1 = ((bf16[16,8,18]{2,1,0:T(8,128)(2,1)}), bf16[16,8,18]{2,1,0:T(8,128)(2,1)}, u32[]{:S(2)}, u32[]{:S(2)}) async-start(bf16[16,8,18]{2,1,0:T(8,128)(2,1)} %bitcast.164), calls=%async_computation.1 | async-start | bytes 65536 | tf_op jit(solution)/shard_map/all_to_all | solution.py:175
Sparse Core Ops, SparseCore 0:
  46.1 24.8 all-gather.3
  154.5 21.0 reduce-scatter.4
  178.7 60.5 reduce-scatter.6
where the time goes:
time: 271 us; the launch traced here: 268 us
  blocking collectives  101 us (37%)
  local copies, waits for them, and re-layouts  46.2 us (17%)
  waiting for transfers between devices  35.5 us (13%)
  other arithmetic  35.2 us (13%)
  matrix products  24.1 us (9%)
  between operations  14.6 us (5%)
  starting transfers between devices  11.4 us (4%)
    psum x2, blocking collectives, by_axis(): x = lax.psum(x, axis)  63.3 us
    all_gather x1, blocking collectives, stacked_from(): blocks = lax.all_gather(blocks, axes[k], axis=0, tiled=True)  37.6 us
    all_gather x1, waiting for transfers between devices, stacked_from(): blocks = lax.all_gather(blocks, axes[k], axis=0, tiled=True)  22.9 us
    dynamic_update_slice x16, local copies, waits for them, and re-layouts, importance_trace_gradients(): lax.scan(backstep, start, (deltas.T, (discount * ratio).T), reverse=True)  20.6 us
    add x16, other arithmetic, backstep(): carry = delta + factor * carry  19.8 us
    dot_general x7, matrix products, contract(): lax.dot_general(left, right, (((1,), (1,)), ((), ())), preferred_element_...  13 us
    reduce_scatter x1, waiting for transfers between devices, reduced_to_own(): blocks = lax.psum_scatter(blocks, axes[k], scatter_dimension=0, tiled=True)  12.6 us
    unnamed x32, local copies, waits for them, and re-layouts  7.75 us
  transfers between devices with their start and end apart: 5, of which 2 were waited for; matrix products, arithmetic and copies ran while one was open for 7% of the time, Pallas kernels for 0%

commit v1 on v0

--- a/solution.py
+++ b/solution.py
@@ -56,7 +56,8 @@
 
 def by_axis(x, axes):
     for axis in axes:
-        x = lax.psum(x, axis)
+        parts = lax.all_gather(x, axis, axis=0, tiled=False)
+        x = parts.sum(axis=0)
     return x
 
 

time: 271 us -> 258 us (0.952)
  the two profiles are of different devices: /device:TPU:1 before, /device:TPU:2 now
where the time goes in v1:
time: 258 us; the launch traced here: 256 us
  blocking collectives  82 us (32%)
  local copies, waits for them, and re-layouts  42.3 us (16%)
  waiting for transfers between devices  41 us (16%)
  other arithmetic  39.8 us (15%)
  matrix products  22.2 us (9%)
  between operations  14.5 us (6%)
  starting transfers between devices  14 us (5%)
    all_gather x1, blocking collectives, stacked_from(): blocks = lax.all_gather(blocks, axes[k], axis=0, tiled=True)  43.3 us
    all_gather x2, blocking collectives, by_axis(): parts = lax.all_gather(x, axis, axis=0, tiled=False)  38.7 us
    dynamic_update_slice x16, local copies, waits for them, and re-layouts, importance_trace_gradients(): lax.scan(backstep, start, (deltas.T, (discount * ratio).T), reverse=True)  20.6 us
    add x16, other arithmetic, backstep(): carry = delta + factor * carry  20.6 us
    all_gather x1, waiting for transfers between devices, stacked_from(): blocks = lax.all_gather(blocks, axes[k], axis=0, tiled=True)  14.9 us
    unnamed x4, waiting for transfers between devices  13.7 us
    dot_general x7, matrix products, contract(): lax.dot_general(left, right, (((1,), (1,)), ((), ())), preferred_element_...  11.6 us
    reduce_scatter x1, waiting for transfers between devices, reduced_to_own(): blocks = lax.psum_scatter(blocks, axes[k], scatter_dimension=0, tiled=True)  11 us
  transfers between devices with their start and end apart: 5, of which 4 were waited for; matrix products, arithmetic and copies ran while one was open for 8% of the time, Pallas kernels for 0%

profile of v1, /device:TPU:2, one launch (start us, length us, event | category | flops | bytes accessed | tf_op | source)
XLA Modules:
  0.0 255.8 jit_solution(6050916328476935447)
XLA Ops:
  8.3 43.3 %all-gather = bf16[16,8,3712]{2,1,0:T(8,128)(2,1)} all-gather(bf16[1,8,3712]{2,1,0:T(8,128)(2,1)S(1)} %convert_element_type.70), channel_id=2, replica_groups=mesh['agent'=16,'dp_0'=16,'dp_1'=2] {'dp_0'}, dimensions={0}, use_global_device_ids=true | all-gather | bytes 1009664 | tf_op jit(solution)/shard_map/all_gather | solution.py:26
  51.7 1.3 convert_element_type.73
  53.8 14.9 %all-gather.8.cloned.1.call-done = bf16[32,8,3712]{2,1,0:T(8,128)(2,1)} async-done(((bf16[16,8,3712]{2,1,0:T(8,128)(2,1)}), bf16[32,8,3712]{2,1,0:T(8,128)(2,1)}) %all-gather.8.cloned.1.call-update) | async-done | bytes 1900560 | tf_op jit(solution)/shard_map/all_gather | solution.py:26
  68.7 1.7 copy.155
  74.8 1.8 fusion.26
  78.6 2.3 fusion.33
  84.1 1.3 fusion.70
  86.0 41.2 %while.17 = (s32[]{:T(128)}, f32[32]{0:T(128)}, f32[16,32]{1,0:T(8,128)}, f32[16,32]{1,0:T(8,128)}, f32[16,32]{1,0:T(8,128)}, /*index=5*/s32[]{:T(128)}, s32[]{:T(128)}, s32[]{:T(128)}) while((s32[]{:T(128)}, f32[32]{0:T(128)}, f32[16,32]{1,0:T(8,128)}, f32[16,32]{1,0:T(8,128)}, f32[16,32]{1,0:T(8,128)}, /*index=5*/s32[]{:T(128)}, ...), condition=%wide.region_4.5_spmd.clone, body=%wide.region_3.4_spmd.clone.sunk | while | flops 100 | bytes 891 | solution.py:110
  87.3 1.3 dynamic_update_slice.12
  89.9 1.3 dynamic_update_slice.12
  92.4 1.3 dynamic_update_slice.12
  95.0 1.3 dynamic_update_slice.12
  97.6 1.3 dynamic_update_slice.12
  100.2 1.3 dynamic_update_slice.12
  102.7 1.3 dynamic_update_slice.12
  105.3 1.3 dynamic_update_slice.12
  107.9 1.3 dynamic_update_slice.12
  110.5 1.3 dynamic_update_slice.12
  113.1 1.3 dynamic_update_slice.12
  115.6 1.3 dynamic_update_slice.12
  127.2 1.3 bitcast_add_fusion
  128.5 1.4 copy.163
  129.9 1.4 concatenate.38
  131.3 1.3 neg.13
  133.3 1.3 fusion.69
  135.4 1.9 fusion.31
  137.3 1.6 copy.164
  140.0 2.1 convolution_convert_fusion.2
  142.2 1.9 fusion.14
  144.0 1.8 copy.168
  145.8 2.1 convolution_convert_fusion
  148.1 1.4 copy.169
  150.3 2.2 fusion.3
  152.5 7.3 %all-to-all-start = ((bf16[16,8,3456]{2,1,0:T(8,128)(2,1)}), bf16[16,8,3456]{2,1,0:T(8,128)(2,1)}, u32[]{:S(2)}, u32[]{:S(2)}) async-start(bf16[16,8,3456]{2,1,0:T(8,128)(2,1)} %fusion.3), calls=%async_computation | async-start | bytes 1769472 | tf_op jit(solution)/shard_map/all_to_all | solution.py:170
  159.9 11.0 %reduce-scatter.5.cloned.1.call-done = bf16[16,8,3712]{2,1,0:T(8,128)(2,1)} async-done(((bf16[32,8,3712]{2,1,0:T(8,128)(2,1)}), bf16[16,8,3712]{2,1,0:T(8,128)(2,1)}) %reduce-scatter.5.cloned.1.call-update) | async-done | bytes 950288 | tf_op jit(solution)/shard_map/reduce_scatter | solution.py:43
  172.2 1.4 all-to-all-done
  173.6 3.1 %fusion.15 = f32[128,256]{1,0:T(8,128)} fusion(bf16[256,3712]{1,0:T(8,128)(2,1)} %bitcast.140, bf16[16,8,3456]{2,1,0:T(8,128)(2,1)} %all-to-all-done), kind=kOutput, calls=%fused_computation.22 | convolution fusion | flops 226525184 | bytes 2785280 | tf_op jit(solution)/shard_map/dot_general | solution.py:65
  176.7 2.0 fusion.20
  178.7 1.4 copy.156
  180.1 6.6 %all-to-all-start.1 = ((bf16[16,8,18]{2,1,0:T(8,128)(2,1)}), bf16[16,8,18]{2,1,0:T(8,128)(2,1)}, u32[]{:S(2)}, u32[]{:S(2)}) async-start(bf16[16,8,18]{2,1,0:T(8,128)(2,1)} %bitcast.148), calls=%async_computation.1 | async-start | bytes 65536 | tf_op jit(solution)/shard_map/all_to_all | solution.py:176
  187.8 35.5 %all-gather.4 = f32[16,19,256]{2,1,0:T(8,128)} all-gather(f32[1,19,256]{2,1,0:T(8,128)S(1)} %convolution_bitcast_fusion), channel_id=4, replica_groups=mesh['agent'=16,'dp_0'=16,'dp_1'=2] {'dp_0'}, dimensions={0}, use_global_device_ids=true | all-gather | bytes 330752 | tf_op jit(solution)/shard_map/all_gather | solution.py:59
  223.3 1.6 reduce_sum.66
  225.0 3.2 %all-gather.5 = f32[2,19,256]{2,1,0:T(8,128)} all-gather(f32[1,19,256]{2,1,0:T(8,128)} %bitcast.149), channel_id=5, replica_groups=mesh['agent'=16,'dp_0'=16,'dp_1'=2] {'dp_1'}, dimensions={0}, use_global_device_ids=true | all-gather | bytes 58368 | tf_op jit(solution)/shard_map/all_gather | solution.py:59
  228.1 1.4 reduce_sum.67
  229.5 1.5 divide_subtract_fusion.1
  231.7 1.5 gather_fusion
  233.8 13.6 %reduce-scatter.7.cloned.1.call-done = bf16[1,8,3712]{2,1,0:T(8,128)(2,1)} async-done(((bf16[16,8,3712]{2,1,0:T(8,128)(2,1)}), bf16[1,8,3712]{2,1,0:T(8,128)(2,1)}) %reduce-scatter.7.cloned.1.call-update) | async-done | bytes 59408
  247.4 1.8 divide_subtract_fusion
  (75 shorter events, 44.4 us)
Async XLA Ops:
  7.2 64.5 %copy-start = (bf16[1,32,16,3456]{3,2,1,0:T(8,128)(2,1)S(1)}, bf16[1,32,16,3456]{3,2,1,0:T(8,128)(2,1)}, u32[]{:S(2)}) copy-start(bf16[1,32,16,3456]{3,2,1,0:T(8,128)(2,1)} %param.17) | copy-start | bytes 10616836
  7.2 61.5 %all-gather.8.cloned.1.call-start = ((), (), s32[]{:S(2)}) async-start(), calls=%async_computation.5 | async-start | bytes 2850816 | tf_op jit(solution)/shard_map/all_gather | solution.py:26
  51.6 119.3 %reduce-scatter.5.cloned.1.call-start = ((), (), s32[]{:S(2)}) async-start(), calls=%async_computation.4 | async-start | bytes 2850816 | tf_op jit(solution)/shard_map/reduce_scatter | solution.py:43
  53.8 24.8 %copy-start.6 = (s32[32,16]{1,0:T(8,128)}, s32[32,16]{1,0:T(8,128)S(1)}, u32[]{:S(2)}) copy-start(s32[32,16]{1,0:T(8,128)S(1)} %copy.157) | copy-start | bytes 6148
  68.7 1.7 copy-start.10
  70.4 2.4 copy-start.4
  72.8 0.8 copy-start.1
  138.9 3.3 %copy-start.2 = (f32[512,256]{1,0:T(8,128)S(1)}, f32[512,256]{1,0:T(8,128)}, u32[]{:S(2)}) copy-start(f32[512,256]{1,0:T(8,128)} %copy-done.1) | copy-start | bytes 1572868
  138.9 3.3 %copy-start.3 = (f32[512,256]{1,0:T(8,128)S(1)}, f32[512,256]{1,0:T(8,128)}, u32[]{:S(2)}) copy-start(f32[512,256]{1,0:T(8,128)} %get-tuple-element.223) | copy-start | bytes 1572868
  145.8 2.1 copy-start.5
  149.5 0.7 copy-start.9
  152.5 21.1 %all-to-all-start = ((bf16[16,8,3456]{2,1,0:T(8,128)(2,1)}), bf16[16,8,3456]{2,1,0:T(8,128)(2,1)}, u32[]{:S(2)}, u32[]{:S(2)}) async-start(bf16[16,8,3456]{2,1,0:T(8,128)(2,1)} %fusion.3), calls=%async_computation | async-start | bytes 1769472 | tf_op jit(solution)/shard_map/all_to_all | solution.py:170
  159.8 87.6 %reduce-scatter.7.cloned.1.call-start = ((), (), s32[]{:S(2)}) async-start(), calls=%async_computation.6 | async-start | bytes 1009664
  170.9 15.8 %copy-start.8 = (bf16[512,1]{0,1:T(2,128)(2,1)S(1)}, bf16[512,1]{0,1:T(2,128)(2,1)}, u32[]{:S(2)}) copy-start(bf16[512,1]{0,1:T(2,128)(2,1)} %concatenate.38) | copy-start | bytes 3076
  172.2 58.9 %copy-start.7 = (f32[32,19]{0,1:T(8,128)S(1)}, f32[32,19]{0,1:T(8,128)}, u32[]{:S(2)}) copy-start(f32[32,19]{0,1:T(8,128)} %fusion.26) | copy-start | bytes 7300
  180.1 51.6 %all-to-all-start.1 = ((bf16[16,8,18]{2,1,0:T(8,128)(2,1)}), bf16[16,8,18]{2,1,0:T(8,128)(2,1)}, u32[]{:S(2)}, u32[]{:S(2)}) async-start(bf16[16,8,18]{2,1,0:T(8,128)(2,1)} %bitcast.148), calls=%async_computation.1 | async-start | bytes 65536 | tf_op jit(solution)/shard_map/all_to_all | solution.py:176
Sparse Core Ops, SparseCore 0:
  51.8 16.9 all-gather.7
  149.6 21.2 reduce-scatter.4
  174.0 73.4 reduce-scatter.6
